TPU v7x, 32 devices: a whole 2x2x4 slice. The times are simulated.
32 devices in a mesh: groups: 2 (over y), fsdp: 2 (over x), expert: 4 (over z), tensor: 2 (over core).
Axes of the slice: x: 2, y: 2, z: 4, core: 2. Of those that a mesh axis runs over, the one named last changes fastest.
Arguments:
- resid: bfloat16 [32, 6144], P(('groups', 'fsdp', 'expert', 'tensor')), parts along dimension 0, may hold values from -24 to 24
- query: bfloat16 [32, 6144], P(('groups', 'fsdp', 'expert', 'tensor')), parts along dimension 0, may hold values from -9 to 9
- cache: bfloat16 [2, 32, 64, 1024], P(None, ('groups', 'fsdp', 'expert', 'tensor')), parts along dimension 1, may hold values from -4 to 4
- new_key_value: bfloat16 [2, 32, 1024], P(None, ('groups', 'fsdp', 'expert', 'tensor')), parts along dimension 1, may hold values from -4 to 4
- lengths: int32 [32], P(('groups', 'fsdp', 'expert', 'tensor')), parts along dimension 0, may hold values from 2 to 64, as said below
- norm_gain: float32 [6144], replicated, may hold values from 0.1 to 1.9
- router_weight: bfloat16 [6144, 4], replicated, may hold values from -0.078125 to 0.078125
- choices: int32 [32, 2], P('groups'), parts along dimension 0, may hold values from 0 to 3, all different within a row; in each aligned block of 16 rows (0 to 15, 16 to 31, ...) at most 10 rows name the same one
- overflow: int32 [32], P('groups'), parts along dimension 0, may hold values 0 or 1
- up_weight: bfloat16 [4, 8192, 6144], P('expert', 'tensor', 'fsdp'), may hold values from -0.078125 to 0.078125
- down_weight: bfloat16 [4, 8192, 6144], P('expert', 'tensor', 'fsdp'), may hold values from -0.0625 to 0.0625
Outputs:
- stream: bfloat16 [32, 6144], P(('groups', 'fsdp', 'expert', 'tensor')), parts along dimension 0
- moe_out: bfloat16 [32, 6144], P(('groups', 'expert', 'tensor'), 'fsdp'), parts along dimension 0
There are 2 independent parts, one for each index of `groups`. A program takes and returns all parts, laid end to end along the dimension named above; an argument that names none is the same for every part. Nothing has to cross between parts.
Inputs may be any that keep to these rules, and one draw needn't show every extreme that they name: `lengths`: at least one row uses all 64 cached positions. `choices`: each row names two different experts; no expert is named by more than 10 of the 16 rows, and one expert is named by exactly 10.
All inputs are finite; a program needn't handle non-finite values.
Results may differ from a plain program's by a relative error of at most 0.0075.
Values may be sent and summed in bfloat16 or wider, within the bound.
A program may use at most 256 MiB of HBM per device.

v0:
```python
import math

import jax
import jax.numpy as jnp
from jax import lax
from jax.sharding import PartitionSpec as P

QUERY_HEADS = 48
KEY_VALUE_HEADS = 8
HEAD_SIZE = 128
CACHE_POSITIONS = 64


def attend(query, cache, new_key_value, lengths):
    count_of_rows = query.shape[0]
    heads_per_group = QUERY_HEADS // KEY_VALUE_HEADS
    inv_root = 1.0 / math.sqrt(HEAD_SIZE)
    query_rows = query.reshape(count_of_rows, KEY_VALUE_HEADS, heads_per_group, HEAD_SIZE)
    resident_keys = cache[0].reshape(count_of_rows, CACHE_POSITIONS, KEY_VALUE_HEADS, HEAD_SIZE)
    resident_values = cache[1].reshape(count_of_rows, CACHE_POSITIONS, KEY_VALUE_HEADS, HEAD_SIZE)
    new_token_key = new_key_value[0].reshape(count_of_rows, KEY_VALUE_HEADS, HEAD_SIZE)
    new_token_value = new_key_value[1].reshape(count_of_rows, KEY_VALUE_HEADS, HEAD_SIZE)
    scores = (
        jnp.einsum("rgqd,rlgd->rgql", query_rows, resident_keys, preferred_element_type=jnp.float32)
        * inv_root
    )
    own_score = (
        jnp.einsum("rgqd,rgd->rgq", query_rows, new_token_key, preferred_element_type=jnp.float32)
        * inv_root
    )
    visible = jnp.arange(CACHE_POSITIONS)[None, :] < lengths[:, None]
    scores = jnp.where(visible[:, None, None, :], scores, -1e30)
    highest = jnp.maximum(jnp.max(scores, axis=-1), own_score)
    raised = jnp.exp(scores - highest[..., None])
    raised_own = jnp.exp(own_score - highest)
    normalizer = jnp.sum(raised, axis=-1) + raised_own
    attn_prob = (raised / normalizer[..., None]).astype(jnp.bfloat16)
    prob_own = (raised_own / normalizer).astype(jnp.bfloat16)
    attended = jnp.einsum(
        "rgql,rlgd->rgqd", attn_prob, resident_values, preferred_element_type=jnp.float32
    )
    attended = (
        attended
        + prob_own.astype(jnp.float32)[..., None]
        * new_token_value.astype(jnp.float32)[:, :, None, :]
    )
    return attended.reshape(count_of_rows, QUERY_HEADS * HEAD_SIZE)


def expert_gate(every_row, router_weight, choices, overflow, my_expert):
    logits = jnp.dot(every_row, router_weight, preferred_element_type=jnp.float32)
    labels = jnp.arange(router_weight.shape[1])
    first_pick = (choices[:, 0:1] == labels[None, :]).astype(jnp.float32)
    second = (choices[:, 1:2] == labels[None, :]).astype(jnp.float32)
    first_logit = jnp.sum(logits * first_pick, axis=-1)
    second_logit = jnp.sum(logits * second, axis=-1)
    first_prob = 1.0 / (1.0 + jnp.exp(second_logit - first_logit))
    kept_share = first_prob * (1.0 - overflow.astype(jnp.float32))
    own_mask = (labels == my_expert).astype(jnp.float32)[None, :]
    return kept_share * jnp.sum(first_pick * own_mask, axis=-1) + (1.0 - kept_share) * jnp.sum(
        second * own_mask, axis=-1
    )


def shards(
    resid,
    query,
    cache,
    new_key_value,
    lengths,
    norm_gain,
    router_weight,
    choices,
    overflow,
    up_weight,
    down_weight,
):
    attended = attend(query, cache, new_key_value, lengths)
    stream = (resid.astype(jnp.float32) + attended).astype(jnp.bfloat16)
    levels = stream.astype(jnp.float32)
    normed = (
        levels * lax.rsqrt(jnp.mean(levels * levels, axis=-1, keepdims=True) + 1e-05) * norm_gain
    ).astype(jnp.bfloat16)
    up_blocks = lax.all_to_all(up_weight, "fsdp", split_axis=1, concat_axis=2, tiled=True)
    every_row = lax.all_gather(normed, ("fsdp", "expert", "tensor"), axis=0, tiled=True)
    my_expert = lax.axis_index("expert")
    gate_mine = expert_gate(every_row, router_weight, choices, overflow, my_expert)
    pre_active = lax.dot_general(
        every_row, up_blocks[0], (((1,), (1,)), ((), ())), preferred_element_type=jnp.float32
    )
    active = jax.nn.silu(pre_active).astype(jnp.bfloat16)
    down_local = down_weight[0]
    partial_value = jnp.dot(
        lax.all_gather(active, "fsdp", axis=1, tiled=True),
        down_local,
        preferred_element_type=jnp.float32,
    )
    weighted = gate_mine[:, None] * partial_value
    combined = lax.psum_scatter(weighted, ("expert", "tensor"), scatter_dimension=0, tiled=True)
    return (stream, combined.astype(jnp.bfloat16))


def solution(mesh):
    return jax.shard_map(
        shards,
        mesh=mesh,
        in_specs=(
            P(("groups", "fsdp", "expert", "tensor"), None),
            P(("groups", "fsdp", "expert", "tensor"), None),
            P(None, ("groups", "fsdp", "expert", "tensor"), None, None),
            P(None, ("groups", "fsdp", "expert", "tensor"), None),
            P(("groups", "fsdp", "expert", "tensor")),
            P(),
            P(),
            P("groups", None),
            P("groups"),
            P("expert", "tensor", "fsdp"),
            P("expert", "tensor", "fsdp"),
        ),
        out_specs=(
            P(("groups", "fsdp", "expert", "tensor"), None),
            P(("groups", "expert", "tensor"), "fsdp"),
        ),
        check_vma=False,
    )
```

profile of v0, /device:TPU:0, one launch (start us, length us, event | category | flops | bytes accessed | tf_op | source)
XLA Modules:
  0.0 696.1 jit_solution(16843534284642918056)
XLA Ops:
  0.6 0.0 copy-start
  0.6 43.4 %copy.45 = bf16[1,4096,3072]{2,0,1:T(2,128)(2,1)} copy(bf16[1,4096,3072]{2,1,0:T(8,128)(2,1)} %param.20) | data formatting | bytes 50331648 | tf_op args[9]
  44.0 0.5 broadcast.49
  44.5 149.4 %reduce.6 = bf16[4096,3072]{1,0:T(8,128)(2,1)} reduce(bf16[4096,1,3072]{2,1,0:T(2,128)(2,1)} %bitcast.53, bf16[]{:T(256)} %broadcast.49), dimensions={1}, to_apply=%bitcast.51.reduce_sub_computation | reduce | bytes 50331648
  193.9 40.3 %reshape.119 = bf16[2,2,3145728]{2,1,0:T(2,128)(2,1)} reshape(bf16[4096,3072]{1,0:T(8,128)(2,1)} %reduce.6) | data formatting | bytes 50331648
  234.2 0.0 copy-start.1
  234.2 0.0 copy-start.3
  234.2 0.0 copy-start.6
  234.2 0.0 copy-start.4
  234.2 0.0 copy-start.9
  234.2 0.0 copy-start.5
  234.2 0.0 copy-start.7
  234.3 0.0 copy-start.8
  234.3 12.0 %all-to-all-start = ((bf16[2,2,3145728]{2,1,0:T(2,128)(2,1)}), bf16[2,2,3145728]{2,1,0:T(2,128)(2,1)}, u32[]{:S(2)}, u32[]{:S(2)}) async-start(bf16[2,2,3145728]{2,1,0:T(2,128)(2,1)} %reshape.119), calls=%async_computation | async-start | bytes 50331648 | tf_op jit(solution)/shard_map/all_to_all | solution.py:84
  246.3 0.0 copy-done.1
  246.4 0.0 copy-done.3
  246.4 0.1 reduce.5
  247.2 0.0 copy-done.6
  247.2 0.1 fusion.19
  247.3 0.2 fusion.24
  247.6 0.2 fusion.16
  247.8 0.2 convolution_add_fusion
  248.0 0.0 copy-done.4
  248.0 0.7 multiply_reduce_fusion
  248.7 0.0 copy-start.2
  249.4 0.0 copy-done.9
  249.4 0.6 dynamic-slice
  250.7 0.0 copy-done.5
  250.7 25.5 %all-gather = bf16[16,1,6144]{2,1,0:T(2,128)(2,1)S(1)} all-gather(bf16[1,1,6144]{2,1,0:T(2,128)(2,1)S(1)} %convert_bitcast_fusion), channel_id=1, replica_groups=mesh['groups'=2,'fsdp'=2,'expert'=4,'tensor'=2] {'fsdp','expert','tensor'}, dimensions={0}, use_global_device_ids=true | all-gather | bytes 208896 | tf_op jit(solution)/shard_map/all_gather | solution.py:85
  276.2 0.0 copy-done.7
  276.2 0.0 copy-done
  276.2 0.2 select_reduce_fusion.2
  276.5 0.0 copy-done.8
  276.5 245.5 %all-to-all-done = bf16[2,2,3145728]{2,1,0:T(2,128)(2,1)} async-done(((bf16[2,2,3145728]{2,1,0:T(2,128)(2,1)}), bf16[2,2,3145728]{2,1,0:T(2,128)(2,1)}, u32[]{:S(2)}, u32[]{:S(2)}) %all-to-all-start) | async-done | bytes 25165856 | tf_op jit(solution)/shard_map/all_to_all | solution.py:84
  521.9 55.5 %reshape.120 = bf16[4096,1,3072]{2,1,0:T(2,128)(2,1)} reshape(bf16[2,2,3145728]{2,1,0:T(2,128)(2,1)} %all-to-all-done) | data formatting | bytes 50331648
  577.5 0.0 copy-done.2
  577.5 31.9 %copy.25 = bf16[1,4096,3072]{2,1,0:T(8,128)(2,1)} copy(bf16[1,4096,3072]{2,0,1:T(2,128)(2,1)} %bitcast.54) | data formatting | bytes 50331648
  609.4 32.7 %copy.21 = bf16[1,2048,2,3072]{1,3,2,0:T(8,128)(2,1)} copy(bf16[1,2048,2,3072]{3,1,2,0:T(8,128)(2,1)} %bitcast.56) | data formatting | bytes 50331648 | tf_op jit(solution)/shard_map/all_to_all | solution.py:84
  642.1 10.0 %multiply_convert_fusion = bf16[16,2048]{1,0:T(8,128)(2,1)S(1)} fusion(bf16[2048,6144]{0,1:T(8,128)(2,1)} %bitcast.55, bf16[16,1,6144]{2,1,0:T(2,128)(2,1)S(1)} %all-gather), kind=kOutput, calls=%fused_computation.12 | convolution fusion | flops 402817024 | bytes 25427968 | tf_op jit(solution)/shard_map/dot_general | solution.py:88
  652.1 4.9 all_gather.7
  657.0 9.9 %fusion.2 = f32[16,3072]{1,0:T(8,128)S(1)} fusion(bf16[16,4096]{1,0:T(8,128)(2,1)S(1)} %all_gather.7, bf16[1,4096,3072]{2,1,0:T(8,128)(2,1)} %param.21, f32[16]{0:T(128)S(1)} %multiply_add_fusion), kind=kOutput, calls=%fused_computation.2 | convolution fusion | flops 402702336 | bytes 25493568 | tf_op jit(solution)/shard_map/dot_general | solution.py:93
  666.9 28.6 %all-reduce.2 = bf16[16,3072]{1,0:T(8,128)(2,1)S(1)} all-reduce(f32[16,3072]{1,0:T(8,128)S(1)} %fusion.2), channel_id=2, replica_groups=mesh['groups'=2,'fsdp'=2,'expert'=4,'tensor'=2] {'expert','tensor'}, use_global_device_ids=true, to_apply=%region_7.8.clone | all-reduce | flops 49152 | bytes 294912
  695.5 0.6 dynamic-slice_convert_fusion
  (13 shorter events, 0.2 us)
Async XLA Ops:
  0.6 275.6 %copy-start = (bf16[6144,4]{0,1:T(4,128)(2,1)S(1)}, bf16[6144,4]{0,1:T(4,128)(2,1)}, u32[]{:S(2)}) copy-start(bf16[6144,4]{0,1:T(4,128)(2,1)} %param.17) | copy-start | bytes 147460
  234.2 12.1 %copy-start.1 = (bf16[2,1,64,1024]{3,2,1,0:T(8,128)(2,1)S(1)}, bf16[2,1,64,1024]{3,2,1,0:T(8,128)(2,1)}, u32[]{:S(2)}) copy-start(bf16[2,1,64,1024]{3,2,1,0:T(8,128)(2,1)} %param.13) | copy-start | bytes 786436
  234.2 12.2 %copy-start.3 = (bf16[1,6144]{1,0:T(2,128)(2,1)S(1)}, bf16[1,6144]{1,0:T(2,128)(2,1)}, u32[]{:S(2)}) copy-start(bf16[1,6144]{1,0:T(2,128)(2,1)} %param.12) | copy-start | bytes 36868
  234.2 13.0 %copy-start.6 = (bf16[2,1,1024]{2,0,1:T(2,128)(2,1)S(1)}, bf16[2,1,1024]{2,0,1:T(2,128)(2,1)}, u32[]{:S(2)}) copy-start(bf16[2,1,1024]{2,0,1:T(2,128)(2,1)} %param.14) | copy-start | bytes 12292
  234.2 13.8 %copy-start.4 = (bf16[1,6144]{1,0:T(2,128)(2,1)S(1)}, bf16[1,6144]{1,0:T(2,128)(2,1)}, u32[]{:S(2)}) copy-start(bf16[1,6144]{1,0:T(2,128)(2,1)} %param.11) | copy-start | bytes 36868
  234.2 15.2 %copy-start.9 = (u32[32]{0:T(128)S(1)}, u32[32]{0:T(128)}, u32[]{:S(2)}) copy-start(u32[32]{0:T(128)} %constant.39) | copy-start | bytes 388
  234.2 16.4 %copy-start.5 = (f32[6144]{0:T(1024)S(1)}, f32[6144]{0:T(1024)}, u32[]{:S(2)}) copy-start(f32[6144]{0:T(1024)} %param.16) | copy-start | bytes 73732
  234.2 41.9 %copy-start.7 = (s32[16,2]{0,1:T(2,128)S(1)}, s32[16,2]{0,1:T(2,128)}, u32[]{:S(2)}) copy-start(s32[16,2]{0,1:T(2,128)} %param.18) | copy-start | bytes 388
  234.3 42.2 %copy-start.8 = (s32[16]{0:T(128)S(1)}, s32[16]{0:T(128)}, u32[]{:S(2)}) copy-start(s32[16]{0:T(128)} %param.19) | copy-start | bytes 196
  234.3 287.7 %all-to-all-start = ((bf16[2,2,3145728]{2,1,0:T(2,128)(2,1)}), bf16[2,2,3145728]{2,1,0:T(2,128)(2,1)}, u32[]{:S(2)}, u32[]{:S(2)}) async-start(bf16[2,2,3145728]{2,1,0:T(2,128)(2,1)} %reshape.119), calls=%async_computation | async-start | bytes 50331648 | tf_op jit(solution)/shard_map/all_to_all | solution.py:84
  248.7 328.8 %copy-start.2 = (bf16[1,6144]{1,0:T(2,128)(2,1)}, bf16[1,6144]{1,0:T(2,128)(2,1)S(1)}, u32[]{:S(2)}) copy-start(bf16[1,6144]{1,0:T(2,128)(2,1)S(1)} %get-tuple-element.7) | copy-start | bytes 36868
where the time goes:
time: 698 us; the launch traced here: 696 us
  waiting for transfers between devices  245 us (35%)
  local copies, waits for them, and re-layouts  206 us (30%)
  other arithmetic  150 us (21%)
  blocking collectives  59 us (8%)
  matrix products  20.7 us (3%)
  starting transfers between devices  12 us (2%)
    all_to_all x1, waiting for transfers between devices, shards(): lax.all_to_all(up_weight, 'fsdp', split_axis=1, concat_axis=2, tiled=True)  245 us
    unnamed x29, local copies, waits for them, and re-layouts  172 us
    unnamed x3, other arithmetic  149 us
    all_to_all x1, local copies, waits for them, and re-layouts, shards(): lax.all_to_all(up_weight, 'fsdp', split_axis=1, concat_axis=2, tiled=True)  32.7 us
    unnamed x1, blocking collectives  28.6 us
    all_gather x1, blocking collectives, shards(): lax.all_gather(normed, ('fsdp', 'expert', 'tensor'), axis=0, tiled=True)  25.5 us
  transfers between devices with their start and end apart: 1, of which 1 were waited for; matrix products, arithmetic and copies ran while one was open for 0% of the time, Pallas kernels for 0%

commit v1 on v0

--- a/solution.py
+++ b/solution.py
@@ -81,18 +81,21 @@
     normed = (
         levels * lax.rsqrt(jnp.mean(levels * levels, axis=-1, keepdims=True) + 1e-05) * norm_gain
     ).astype(jnp.bfloat16)
-    up_blocks = lax.all_to_all(up_weight, "fsdp", split_axis=1, concat_axis=2, tiled=True)
     every_row = lax.all_gather(normed, ("fsdp", "expert", "tensor"), axis=0, tiled=True)
     my_expert = lax.axis_index("expert")
     gate_mine = expert_gate(every_row, router_weight, choices, overflow, my_expert)
-    pre_active = lax.dot_general(
-        every_row, up_blocks[0], (((1,), (1,)), ((), ())), preferred_element_type=jnp.float32
+    features = up_weight.shape[2]
+    my_features = lax.dynamic_slice_in_dim(
+        every_row, lax.axis_index("fsdp") * features, features, axis=1
     )
+    partial_active = lax.dot_general(
+        my_features, up_weight[0], (((1,), (1,)), ((), ())), preferred_element_type=jnp.float32
+    )
+    pre_active = lax.psum_scatter(partial_active, "fsdp", scatter_dimension=1, tiled=True)
     active = jax.nn.silu(pre_active).astype(jnp.bfloat16)
-    down_local = down_weight[0]
     partial_value = jnp.dot(
         lax.all_gather(active, "fsdp", axis=1, tiled=True),
-        down_local,
+        down_weight[0],
         preferred_element_type=jnp.float32,
     )
     weighted = gate_mine[:, None] * partial_value

time: 698 us -> 115 us (0.16)
  waiting for transfers between devices: 245 us -> 7.56 us
  local copies, waits for them, and re-layouts: 206 us -> 2.52 us
  other arithmetic: 150 us -> 4.86 us
  between operations: 2.87 us -> 16.2 us
  starting transfers between devices: 12 us -> 0.04 us
    all_to_all x1 -> x0, waiting for transfers between devices: 245 us -> none  [shards(): lax.all_to_all(up_weight, 'fsdp', split_axis=1, concat_axis=2, tiled=True)]
    unnamed x29 -> x14, local copies, waits for them, and re-layouts: 172 us -> 1.65 us
    unnamed x3 -> x2, other arithmetic: 149 us -> 1.59 us
    all_to_all x1 -> x0, local copies, waits for them, and re-layouts: 32.7 us -> none  [shards(): lax.all_to_all(up_weight, 'fsdp', split_axis=1, concat_axis=2, tiled=True)]
    all_to_all x1 -> x0, starting transfers between devices: 12 us -> none  [shards(): lax.all_to_all(up_weight, 'fsdp', split_axis=1, concat_axis=2, tiled=True)]
    reduce_scatter x0 -> x1, waiting for transfers between devices: none -> 7.54 us  [shards(): lax.psum_scatter(partial_active, 'fsdp', scatter_dimension=1, tiled=True)]
  transfers between devices with their start and end apart: 1 -> 1, of which waited for: 1 -> 1; matrix products, arithmetic and copies ran while one was open for 0% -> 1% of each run, Pallas kernels for 0% -> 0%
where the time goes in v1:
time: 115 us; the launch traced here: 114 us
  blocking collectives  59.4 us (52%)
  matrix products  23.6 us (21%)
  between operations  16.2 us (14%)
  waiting for transfers between devices  7.56 us (7%)
  other arithmetic  4.86 us (4%)
  local copies, waits for them, and re-layouts  2.52 us (2%)
    unnamed x1, blocking collectives  29.7 us
    all_gather x1, blocking collectives, shards(): lax.all_gather(normed, ('fsdp', 'expert', 'tensor'), axis=0, tiled=True)  24.8 us
    dot_general x1, matrix products, shards(): lax.dot_general(my_features, up_weight[0], (((1,), (1,)), ((), ())), pref...  12.2 us
    dot_general x1, matrix products, shards(): jnp.dot(lax.all_gather(active, 'fsdp', axis=1, tiled=True), down_weight[0...  9.88 us
    reduce_scatter x1, waiting for transfers between devices, shards(): lax.psum_scatter(partial_active, 'fsdp', scatter_dimension=1, tiled=True)  7.54 us
    all_gather x1, blocking collectives, shards(): lax.all_gather(active, 'fsdp', axis=1, tiled=True)  4.94 us
  transfers between devices with their start and end apart: 1, of which 1 were waited for; matrix products, arithmetic and copies ran while one was open for 1% of the time, Pallas kernels for 0%

profile of v1, /device:TPU:0, one launch (start us, length us, event | category | flops | bytes accessed | tf_op | source)
XLA Modules:
  0.0 114.2 jit_solution(14470126801547832566)
XLA Ops:
  7.2 0.0 copy-start
  7.2 0.0 copy-start.4
  7.2 0.0 copy-start.2
  7.2 0.0 copy-start.3
  7.2 0.0 reduce-scatter.2.cloned.1.call-start
  7.3 1.0 slice_bitcast_fusion.1
  8.3 0.8 reduce.5
  9.8 0.7 slice_convert_fusion
  10.5 0.8 fusion.16
  11.3 0.2 fusion.21
  11.5 0.2 fusion.13
  11.8 0.2 convolution_add_fusion
  12.0 1.4 %multiply_reduce_fusion = (f32[]{:T(128)}, bf16[1,6144]{1,0:T(2,128)(2,1)S(1)}) fusion(f32[1,6144]{1,0:T(1,128)S(1)} %reshape.109, bf16[1,6144]{1,0:T(2,128)(2,1)} %param.11), kind=kLoop, calls=%fused_computation.22 | loop fusion | flops 36863 | bytes 49156 | tf_op jit(solution)/shard_map/reduce_sum | solution.py:82
  13.4 0.0 copy-start.1
  14.1 0.8 convert_bitcast_fusion
  14.9 24.8 %all-gather = bf16[16,1,6144]{2,1,0:T(2,128)(2,1)S(1)} all-gather(bf16[1,1,6144]{2,1,0:T(2,128)(2,1)S(1)} %convert_bitcast_fusion), channel_id=1, replica_groups=mesh['groups'=2,'fsdp'=2,'expert'=4,'tensor'=2] {'fsdp','expert','tensor'}, dimensions={0}, use_global_device_ids=true | all-gather | bytes 208896 | tf_op jit(solution)/shard_map/all_gather | solution.py:84
  39.7 0.2 constant_dynamic-slice_fusion
  39.9 12.2 %fusion.2 = f32[16,4096]{1,0:T(8,128)} fusion(bf16[1,4096,3072]{2,1,0:T(8,128)(2,1)} %param.20, bf16[16,1,3072]{2,1,0:T(2,128)(2,1)S(1)} %constant_dynamic-slice_fusion), kind=kOutput, calls=%fused_computation.2 | convolution fusion | flops 402653184 | bytes 25526272 | tf_op jit(solution)/shard_map/dot_general | solution.py:91
  52.1 0.0 reduce-scatter.2.cloned.1.call-update
  52.2 0.0 copy-done.4
  52.2 0.6 dynamic-slice.1
  53.4 0.0 copy-done.2
  53.4 0.0 copy-done
  53.4 0.2 select_reduce_fusion.2
  53.7 0.0 copy-done.3
  53.7 7.5 %reduce-scatter.2.cloned.1.call-done = f32[16,2048]{1,0:T(8,128)} async-done(((f32[16,4096]{1,0:T(8,128)}), f32[16,2048]{1,0:T(8,128)}) %reduce-scatter.2.cloned.1.call-update) | async-done | bytes 131088 | tf_op jit(solution)/shard_map/reduce_scatter | solution.py:94
  61.3 0.9 multiply_convert_fusion
  62.2 4.9 %all_gather.7 = bf16[16,4096]{1,0:T(8,128)(2,1)S(1)} all-gather(bf16[16,2048]{1,0:T(8,128)(2,1)S(1)} %multiply_convert_fusion), channel_id=1, replica_groups=mesh['groups'=2,'fsdp'=2,'expert'=4,'tensor'=2] {'fsdp'}, dimensions={1}, use_global_device_ids=true | all-gather | bytes 196608 | tf_op jit(solution)/shard_map/all_gather | solution.py:97
  67.2 9.9 %fusion.4 = f32[16,3072]{1,0:T(8,128)S(1)} fusion(bf16[16,4096]{1,0:T(8,128)(2,1)S(1)} %all_gather.7, bf16[1,4096,3072]{2,1,0:T(8,128)(2,1)} %param.21, f32[16]{0:T(128)S(1)} %multiply_add_fusion), kind=kOutput, calls=%fused_computation.4 | convolution fusion | flops 402702336 | bytes 25493568 | tf_op jit(solution)/shard_map/dot_general | solution.py:96
  77.0 0.0 copy-done.1
  77.0 29.7 %all-reduce.2 = bf16[16,3072]{1,0:T(8,128)(2,1)S(1)} all-reduce(f32[16,3072]{1,0:T(8,128)S(1)} %fusion.4), channel_id=3, replica_groups=mesh['groups'=2,'fsdp'=2,'expert'=4,'tensor'=2] {'expert','tensor'}, use_global_device_ids=true, to_apply=%region_8.9.clone | all-reduce | flops 49152 | bytes 294912
  106.7 0.6 dynamic-slice_convert_fusion
  (10 shorter events, 0.1 us)
Async XLA Ops:
  7.2 46.3 %copy-start = (bf16[6144,4]{0,1:T(4,128)(2,1)S(1)}, bf16[6144,4]{0,1:T(4,128)(2,1)}, u32[]{:S(2)}) copy-start(bf16[6144,4]{0,1:T(4,128)(2,1)} %param.17) | copy-start | bytes 147460
  7.2 45.0 %copy-start.4 = (u32[32]{0:T(128)S(1)}, u32[32]{0:T(128)}, u32[]{:S(2)}) copy-start(u32[32]{0:T(128)} %constant.49) | copy-start | bytes 388
  7.2 46.2 %copy-start.2 = (s32[16,2]{0,1:T(2,128)S(1)}, s32[16,2]{0,1:T(2,128)}, u32[]{:S(2)}) copy-start(s32[16,2]{0,1:T(2,128)} %param.18) | copy-start | bytes 388
  7.2 46.5 %copy-start.3 = (s32[16]{0:T(128)S(1)}, s32[16]{0:T(128)}, u32[]{:S(2)}) copy-start(s32[16]{0:T(128)} %param.19) | copy-start | bytes 196
  7.2 54.0 %reduce-scatter.2.cloned.1.call-start = ((), (), s32[]{:S(2)}) async-start(), calls=%async_computation.1 | async-start | bytes 393216 | tf_op jit(solution)/shard_map/reduce_scatter | solution.py:94
  13.4 63.6 %copy-start.1 = (bf16[1,6144]{1,0:T(2,128)(2,1)}, bf16[1,6144]{1,0:T(2,128)(2,1)S(1)}, u32[]{:S(2)}) copy-start(bf16[1,6144]{1,0:T(2,128)(2,1)S(1)} %get-tuple-element.7) | copy-start | bytes 36868
Sparse Core Ops, SparseCore 0:
  52.3 8.9 reduce-scatter.1

commit v2 on v1

--- a/solution.py
+++ b/solution.py
@@ -3,6 +3,8 @@
 import jax
 import jax.numpy as jnp
 from jax import lax
+from jax.experimental import pallas as pl
+from jax.experimental.pallas import tpu as pltpu
 from jax.sharding import PartitionSpec as P
 
 QUERY_HEADS = 48
@@ -103,9 +105,490 @@
     return (stream, combined.astype(jnp.bfloat16))
 
 
+MESH = pl.DeviceIdType.MESH
+GROUPS, FSDP, EXPERTS, CORES = 2, 2, 4, 2
+PLANE = FSDP * EXPERTS
+BLOCKS = GROUPS * CORES
+ROWS = BLOCKS * PLANE
+UP_CHUNKS = 4
+OUT_CHUNKS = 3
+
+
+def place_of(slot):
+    block, inner = divmod(slot, PLANE)
+    group, core = divmod(block, CORES)
+    row = inner * CORES + core
+    expert_to, rest = divmod(row, 4)
+    core_to, pair = divmod(rest, 2)
+    return group * 16 + core_to * 8 + expert_to * 2 + pair
+
+
+def layer_kernel(
+    lengths,
+    choices,
+    overflow,
+    resid,
+    query,
+    new_kv,
+    gain,
+    cache,
+    router,
+    up,
+    down,
+    stream_out,
+    moe_out,
+    kv,
+    rt,
+    upw,
+    downw,
+    qbd,
+    r48,
+    payload,
+    rows_in,
+    rows_all,
+    xs,
+    x,
+    meta,
+    logit_mine,
+    logit_in,
+    pre_mine,
+    pre_send,
+    pre_in,
+    act,
+    acc,
+    own_out,
+    a_send,
+    a_in,
+    z_send,
+    z_in,
+    local_sem,
+    up_sem,
+    down_sem,
+    row_send_sem,
+    row_recv_sem,
+    block_send_sem,
+    block_recv_sem,
+    pair_send_sem,
+    pair_recv_sem,
+    pre_send_sem,
+    pre_recv_sem,
+    a_send_sem,
+    a_recv_sem,
+    z_send_sem,
+    z_recv_sem,
+):
+    g = lax.axis_index("groups")
+    f = lax.axis_index("fsdp")
+    e = lax.axis_index("expert")
+    t = lax.axis_index("tensor")
+    here = f * EXPERTS + e
+    block = g * CORES + t
+    features = x.shape[1]
+    pieces = features // HEAD_SIZE
+    heads = 2 * pieces
+    group_heads = heads // KEY_VALUE_HEADS
+    hidden = upw.shape[1]
+    width = moe_out.shape[1] // OUT_CHUNKS
+    half = width // 2
+
+    def remote(src, dst, send, recv, device):
+        return pltpu.make_async_remote_copy(
+            src_ref=src,
+            dst_ref=dst,
+            send_sem=send,
+            recv_sem=recv,
+            device_id=device,
+            device_id_type=MESH,
+        )
+
+    def plane_peer(k):
+        other = lax.rem(here + k, PLANE)
+        return other // EXPERTS, lax.rem(other, EXPERTS)
+
+    def block_peer(k):
+        other = lax.rem(block + k, BLOCKS)
+        return other, other // CORES, lax.rem(other, CORES)
+
+    key_copy = pltpu.make_async_copy(cache.at[0, 0], kv.at[0], local_sem.at[0])
+    value_copy = pltpu.make_async_copy(cache.at[1, 0], kv.at[1], local_sem.at[1])
+    key_copy.start()
+    value_copy.start()
+
+    barrier = pltpu.get_barrier_semaphore()
+    for k in range(1, PLANE):
+        f2, e2 = plane_peer(k)
+        pl.semaphore_signal(barrier, inc=1, device_id=(g, f2, e2, t), device_id_type=MESH)
+    for k in range(1, BLOCKS):
+        _, g2, t2 = block_peer(k)
+        pl.semaphore_signal(barrier, inc=1, device_id=(g2, f, e, t2), device_id_type=MESH)
+
+    router_copy = pltpu.make_async_copy(
+        router.at[pl.ds(pl.multiple_of(f * features, features), features), :], rt, local_sem.at[2]
+    )
+
+    def up_copy(c):
+        start = pl.multiple_of(g * (UP_CHUNKS * hidden) + c * hidden, hidden)
+        return pltpu.make_async_copy(up.at[0, pl.ds(start, hidden), :], upw.at[c], up_sem.at[c])
+
+    def down_copy(c):
+        start = pl.multiple_of(g * (UP_CHUNKS * hidden) + c * hidden, hidden)
+        return pltpu.make_async_copy(
+            down.at[0, pl.ds(start, hidden), :],
+            downw.at[pl.ds(c * hidden, hidden), :],
+            down_sem.at[c],
+        )
+
+    router_copy.start()
+    for c in range(UP_CHUNKS):
+        up_copy(c).start()
+    for c in range(UP_CHUNKS):
+        down_copy(c).start()
+
+    qbd[...] = jnp.zeros_like(qbd)
+    query_row = query[...].astype(jnp.float32)
+    resid_row = resid[...].astype(jnp.float32)
+    for h in range(heads):
+        kv_at = h // group_heads * HEAD_SIZE
+        qbd[h : h + 1, kv_at : kv_at + HEAD_SIZE] = query_row[:, h * HEAD_SIZE : (h + 1) * HEAD_SIZE]
+        r48[h : h + 1, :] = resid_row[:, h * HEAD_SIZE : (h + 1) * HEAD_SIZE]
+    inv_root = 1.0 / math.sqrt(HEAD_SIZE)
+    new_key = new_kv[0].astype(jnp.float32)
+    new_value = new_kv[1].astype(jnp.float32)
+    spread = qbd[...]
+    own_score = jnp.sum(spread * new_key, axis=-1, keepdims=True) * inv_root
+    spread = spread.astype(jnp.bfloat16)
+    key_copy.wait()
+    scores = (
+        lax.dot_general(
+            spread, kv[0], (((1,), (1,)), ((), ())), preferred_element_type=jnp.float32
+        )
+        * inv_root
+    )
+    position = lax.broadcasted_iota(jnp.int32, scores.shape, 1)
+    scores = jnp.where(position < lengths[0], scores, -1e30)
+    highest = jnp.maximum(jnp.max(scores, axis=-1, keepdims=True), own_score)
+    raised = jnp.exp(scores - highest)
+    raised_own = jnp.exp(own_score - highest)
+    normalizer = jnp.sum(raised, axis=-1, keepdims=True) + raised_own
+    attn_prob = (raised / normalizer).astype(jnp.bfloat16)
+    prob_own = (raised_own / normalizer).astype(jnp.bfloat16).astype(jnp.float32)
+    value_copy.wait()
+    mixed = jnp.dot(attn_prob, kv[1], preferred_element_type=jnp.float32) + prob_own * new_value
+    head_at = lax.broadcasted_iota(jnp.int32, (heads, HEAD_SIZE), 0)
+    attended = mixed[:, :HEAD_SIZE]
+    for group in range(1, KEY_VALUE_HEADS):
+        attended = jnp.where(
+            head_at >= group * group_heads,
+            mixed[:, group * HEAD_SIZE : (group + 1) * HEAD_SIZE],
+            attended,
+        )
+    levels = (r48[...] + attended).astype(jnp.bfloat16).astype(jnp.float32)
+    total = jnp.sum(jnp.sum(levels * levels, axis=1, keepdims=True), axis=0, keepdims=True)
+    normed = levels * lax.rsqrt(total / (heads * HEAD_SIZE) + 1e-05) * gain[...]
+    filler = jnp.zeros((payload.shape[1] - pieces, HEAD_SIZE), jnp.float32)
+    for part in range(FSDP):
+        payload[part] = jnp.concatenate(
+            [normed[part * pieces : (part + 1) * pieces], filler], axis=0
+        ).astype(jnp.bfloat16)
+
+    pl.semaphore_wait(barrier, PLANE - 1 + BLOCKS - 1)
+
+    row_copies = []
+    for k in range(1, PLANE):
+        f2, e2 = plane_peer(k)
+        row_copies.append(
+            remote(
+                payload.at[f2],
+                rows_in.at[here],
+                row_send_sem.at[k - 1],
+                row_recv_sem.at[k - 1],
+                (g, f2, e2, t),
+            )
+        )
+        row_copies[-1].start()
+    rows_in[here] = payload[f]
+
+    for h in range(heads):
+        stream_out[:, h * HEAD_SIZE : (h + 1) * HEAD_SIZE] = levels[h : h + 1].astype(jnp.bfloat16)
+
+    at = lax.broadcasted_iota(jnp.int32, (16, HEAD_SIZE), 0)
+    lane = lax.broadcasted_iota(jnp.int32, (16, HEAD_SIZE), 1)
+    facts = jnp.zeros((16, HEAD_SIZE), jnp.float32)
+    for row in range(16):
+        place = row % 4 // 2 * 8 + row // 4 * 2 + row % 2
+        for col, value in enumerate((choices[row, 0], choices[row, 1], overflow[row])):
+            facts = jnp.where((at == place) & (lane == col), value.astype(jnp.float32), facts)
+    meta[g] = facts
+    meta_copy = remote(
+        meta.at[g], meta.at[g], pair_send_sem.at[0], pair_recv_sem.at[0], (1 - g, f, e, t)
+    )
+    meta_copy.start()
+
+    for copy in row_copies:
+        copy.wait_recv()
+    mine = rows_in[...].astype(jnp.float32)[:, :pieces]
+    rows_all[block] = mine.reshape(PLANE * pieces, HEAD_SIZE).astype(jnp.bfloat16)
+    block_copies = []
+    for k in range(1, BLOCKS):
+        _, g2, t2 = block_peer(k)
+        block_copies.append(
+            remote(
+                rows_all.at[block],
+                rows_all.at[block],
+                block_send_sem.at[k - 1],
+                block_recv_sem.at[k - 1],
+                (g2, f, e, t2),
+            )
+        )
+        block_copies[-1].start()
+    for copy in block_copies:
+        copy.wait_recv()
+
+    for b in range(BLOCKS):
+        taken = rows_all[b].astype(jnp.float32)
+        for i in range(PLANE):
+            to = place_of(b * PLANE + i) * pieces
+            xs[to : to + pieces, :] = taken[i * pieces : (i + 1) * pieces]
+    for j in range(pieces):
+        x[:, j * HEAD_SIZE : (j + 1) * HEAD_SIZE] = xs[pl.ds(j, ROWS, stride=pieces), :].astype(
+            jnp.bfloat16
+        )
+
+    across = (g, 1 - f, e, t)
+    router_copy.wait()
+    labels = rt.shape[1]
+    logit_mine[...] = jnp.zeros_like(logit_mine)
+    logit_mine[:, :labels] = jnp.dot(x[...], rt[...], preferred_element_type=jnp.float32)
+    logit_copy = remote(logit_mine, logit_in, pair_send_sem.at[1], pair_recv_sem.at[1], across)
+    logit_copy.start()
+
+    def pre_copy(c):
+        return remote(
+            pre_send.at[c], pre_in.at[c], pre_send_sem.at[c], pre_recv_sem.at[c], across
+        )
+
+    def up_step(c, carry):
+        up_copy(c).wait()
+        partial = lax.dot_general(
+            x[...], upw[c], (((1,), (1,)), ((), ())), preferred_element_type=jnp.float32
+        )
+        pre_mine[c] = partial
+        pre_send[c] = partial.astype(jnp.bfloat16)
+        pre_copy(c).start()
+        return carry
+
+    lax.fori_loop(0, UP_CHUNKS, up_step, 0)
+
+    meta_copy.wait_recv()
+    logit_copy.wait_recv()
+    logits = logit_mine[...] + logit_in[...]
+    named = jnp.concatenate([meta[0], meta[1]], axis=0)
+    label = lax.broadcasted_iota(jnp.int32, logits.shape, 1).astype(jnp.float32)
+    first, second, full = named[:, 0:1], named[:, 1:2], named[:, 2:3]
+    first_logit = jnp.sum(jnp.where(label == first, logits, 0.0), axis=1, keepdims=True)
+    second_logit = jnp.sum(jnp.where(label == second, logits, 0.0), axis=1, keepdims=True)
+    first_prob = 1.0 / (1.0 + jnp.exp(second_logit - first_logit))
+    kept = first_prob * (1.0 - full)
+    my_label = e.astype(jnp.float32)
+    gate = jnp.where(first == my_label, kept, 0.0) + jnp.where(second == my_label, 1.0 - kept, 0.0)
+
+    for c in range(UP_CHUNKS):
+        down_copy(c).wait()
+
+    def activate(c):
+        pre_copy(c).wait_recv()
+        value = pre_mine[c] + pre_in[c].astype(jnp.float32)
+        act[:, c * hidden : (c + 1) * hidden] = (value / (1.0 + jnp.exp(-value))).astype(
+            jnp.bfloat16
+        )
+
+    split = UP_CHUNKS // 2 * hidden
+    for c in range(UP_CHUNKS // 2):
+        activate(c)
+    for n in range(OUT_CHUNKS):
+        cols = slice(n * width, (n + 1) * width)
+        acc[:, cols] = jnp.dot(
+            act[:, :split], downw[:split, cols], preferred_element_type=jnp.float32
+        )
+    for c in range(UP_CHUNKS // 2, UP_CHUNKS):
+        activate(c)
+
+    a_copies = [[] for _ in range(OUT_CHUNKS)]
+    z_copies = [[] for _ in range(OUT_CHUNKS)]
+
+    def multiply(n):
+        cols = slice(n * width, (n + 1) * width)
+        value = gate * (
+            acc[:, cols]
+            + jnp.dot(act[:, split:], downw[split:, cols], preferred_element_type=jnp.float32)
+        )
+        for b in range(BLOCKS):
+            rows = value[b * PLANE : (b + 1) * PLANE]
+            folded = jnp.concatenate([rows[:, :half], rows[:, half:]], axis=0)
+            own_out[b] = folded
+            a_send[n, b] = folded.astype(jnp.bfloat16)
+        acc[0:16, n * width : n * width + half] = own_out[block]
+        for k in range(1, BLOCKS):
+            b2, g2, t2 = block_peer(k)
+            at_sem = n * (BLOCKS - 1) + k - 1
+            a_copies[n].append(
+                remote(
+                    a_send.at[n, b2],
+                    a_in.at[n, k - 1],
+                    a_send_sem.at[at_sem],
+                    a_recv_sem.at[at_sem],
+                    (g2, f, e, t2),
+                )
+            )
+            a_copies[n][-1].start()
+
+    def add_blocks(n):
+        value = acc[0:16, n * width : n * width + half]
+        for k in range(1, BLOCKS):
+            a_copies[n][k - 1].wait_recv()
+            value = value + a_in[n, k - 1].astype(jnp.float32)
+        for to in range(EXPERTS):
+            z_send[n, to, :, :half] = value[2 * to : 2 * to + 2]
+            z_send[n, to, :, half:] = value[PLANE + 2 * to : PLANE + 2 * to + 2]
+        for k in range(1, EXPERTS):
+            e2 = lax.rem(e + k, EXPERTS)
+            at_sem = n * (EXPERTS - 1) + k - 1
+            z_copies[n].append(
+                remote(
+                    z_send.at[n, e2],
+                    z_in.at[n, k - 1],
+                    z_send_sem.at[at_sem],
+                    z_recv_sem.at[at_sem],
+                    (g, f, e2, t),
+                )
+            )
+            z_copies[n][-1].start()
+
+    for n in range(OUT_CHUNKS):
+        multiply(n)
+        if n > 0:
+            add_blocks(n - 1)
+    add_blocks(OUT_CHUNKS - 1)
+    for n in range(OUT_CHUNKS):
+        value = z_send[n, e]
+        for k in range(1, EXPERTS):
+            z_copies[n][k - 1].wait_recv()
+            value = value + z_in[n, k - 1]
+        moe_out[:, n * width : (n + 1) * width] = value.astype(jnp.bfloat16)
+
+    for copy in row_copies + block_copies + [meta_copy, logit_copy]:
+        copy.wait_send()
+    for c in range(UP_CHUNKS):
+        pre_copy(c).wait_send()
+    for n in range(OUT_CHUNKS):
+        for copy in a_copies[n] + z_copies[n]:
+            copy.wait_send()
+
+
+def kernel_shards(
+    resid,
+    query,
+    cache,
+    new_key_value,
+    lengths,
+    norm_gain,
+    router_weight,
+    choices,
+    overflow,
+    up_weight,
+    down_weight,
+):
+    _, hidden_all, features = up_weight.shape
+    hidden = hidden_all // GROUPS
+    chunk = hidden // UP_CHUNKS
+    width = features // OUT_CHUNKS
+    pieces = features // HEAD_SIZE
+    padded = -(-pieces // 16) * 16
+    heads = FSDP * pieces
+    kv_features = cache.shape[3]
+    f32, bf16 = jnp.float32, jnp.bfloat16
+    vmem = pl.BlockSpec(memory_space=pltpu.VMEM)
+    smem = pl.BlockSpec(memory_space=pltpu.SMEM)
+    anywhere = pl.BlockSpec(memory_space=pl.ANY)
+    dma = pltpu.SemaphoreType.DMA
+    return pl.pallas_call(
+        layer_kernel,
+        out_shape=(
+            jax.ShapeDtypeStruct(resid.shape, bf16),
+            jax.ShapeDtypeStruct((ROWS // (BLOCKS * EXPERTS), features), bf16),
+        ),
+        in_specs=[smem] * 3 + [vmem] * 4 + [anywhere] * 4,
+        out_specs=(vmem, vmem),
+        scratch_shapes=[
+            pltpu.VMEM((2, CACHE_POSITIONS, kv_features), bf16),
+            pltpu.VMEM((features, router_weight.shape[1]), bf16),
+            pltpu.VMEM((UP_CHUNKS, chunk, features), bf16),
+            pltpu.VMEM((hidden, features), bf16),
+            pltpu.VMEM((heads, kv_features), f32),
+            pltpu.VMEM((heads, HEAD_SIZE), f32),
+            pltpu.VMEM((FSDP, padded, HEAD_SIZE), bf16),
+            pltpu.VMEM((PLANE, padded, HEAD_SIZE), bf16),
+            pltpu.VMEM((BLOCKS, PLANE * pieces, HEAD_SIZE), bf16),
+            pltpu.VMEM((ROWS * pieces, HEAD_SIZE), f32),
+            pltpu.VMEM((ROWS, features), bf16),
+            pltpu.VMEM((GROUPS, 16, HEAD_SIZE), f32),
+            pltpu.VMEM((ROWS, HEAD_SIZE), f32),
+            pltpu.VMEM((ROWS, HEAD_SIZE), f32),
+            pltpu.VMEM((UP_CHUNKS, ROWS, chunk), f32),
+            pltpu.VMEM((UP_CHUNKS, ROWS, chunk), bf16),
+            pltpu.VMEM((UP_CHUNKS, ROWS, chunk), bf16),
+            pltpu.VMEM((ROWS, hidden), bf16),
+            pltpu.VMEM((ROWS, features), f32),
+            pltpu.VMEM((BLOCKS, 16, width // 2), f32),
+            pltpu.VMEM((OUT_CHUNKS, BLOCKS, 16, width // 2), bf16),
+            pltpu.VMEM((OUT_CHUNKS, BLOCKS - 1, 16, width // 2), bf16),
+            pltpu.VMEM((OUT_CHUNKS, EXPERTS, 2, width), f32),
+            pltpu.VMEM((OUT_CHUNKS, EXPERTS - 1, 2, width), f32),
+            dma((3,)),
+            dma((UP_CHUNKS,)),
+            dma((UP_CHUNKS,)),
+            dma((PLANE - 1,)),
+            dma((PLANE - 1,)),
+            dma((BLOCKS - 1,)),
+            dma((BLOCKS - 1,)),
+            dma((2,)),
+            dma((2,)),
+            dma((UP_CHUNKS,)),
+            dma((UP_CHUNKS,)),
+            dma((OUT_CHUNKS * (BLOCKS - 1),)),
+            dma((OUT_CHUNKS * (BLOCKS - 1),)),
+            dma((OUT_CHUNKS * (EXPERTS - 1),)),
+            dma((OUT_CHUNKS * (EXPERTS - 1),)),
+        ],
+        compiler_params=pltpu.CompilerParams(
+            collective_id=0, has_side_effects=True, vmem_limit_bytes=48 * 1024 * 1024
+        ),
+        cost_estimate=pl.CostEstimate(
+            flops=4 * ROWS * hidden * features,
+            bytes_accessed=4 * hidden * features,
+            transcendentals=ROWS * hidden,
+        ),
+        name="layer",
+    )(
+        lengths,
+        choices,
+        overflow,
+        resid,
+        query,
+        new_key_value,
+        norm_gain.reshape(heads, HEAD_SIZE),
+        cache,
+        router_weight,
+        up_weight,
+        down_weight,
+    )
+
+
 def solution(mesh):
+    sizes = tuple(mesh.shape[name] for name in ("groups", "fsdp", "expert", "tensor"))
+    in_kernel = sizes == (GROUPS, FSDP, EXPERTS, CORES)
     return jax.shard_map(
-        shards,
+        kernel_shards if in_kernel else shards,
         mesh=mesh,
         in_specs=(
             P(("groups", "fsdp", "expert", "tensor"), None),

time: 115 us -> 43 us (0.37)
  blocking collectives: 59.4 us -> 0 us
  Pallas kernels: 0 us -> 33.2 us
  matrix products: 23.6 us -> 0 us
  between operations: 16.2 us -> 1.31 us
  waiting for transfers between devices: 7.56 us -> 0 us
  local copies, waits for them, and re-layouts: 2.52 us -> 8.05 us
  other arithmetic: 4.86 us -> 0 us
    pallas_call x0 -> x1, Pallas kernels: none -> 33.2 us  [kernel_shards(): pl.pallas_call(layer_kernel, out_shape=(jax.ShapeDtypeStruct(resid.shape,...]
    all_gather x2 -> x0, blocking collectives: 29.7 us -> none  [the longest x1 24.8 us: shards(): lax.all_gather(normed, ('fsdp', 'expert', 'tensor'), axis=0, tiled=True)]
    unnamed x1 -> x0, blocking collectives: 29.7 us -> none
    dot_general x6 -> x0, matrix products: 23.6 us -> none  [the longest x1 12.2 us: shards(): lax.dot_general(my_features, up_weight[0], (((1,), (1,)), ((), ())), pref...]
    reduce_scatter x1 -> x0, waiting for transfers between devices: 7.54 us -> none  [shards(): lax.psum_scatter(partial_active, 'fsdp', scatter_dimension=1, tiled=True)]
    unnamed x14 -> x15, local copies, waits for them, and re-layouts: 1.65 us -> 8.05 us
    convert_element_type x3 -> x0, other arithmetic: 1.65 us -> none  [the longest x1 0.95 us: shards(): active = jax.nn.silu(pre_active).astype(jnp.bfloat16)]
    unnamed x2 -> x0, other arithmetic: 1.59 us -> none
  transfers between devices with their start and end apart: 1 -> 0, of which waited for: 1 -> 0; matrix products, arithmetic and copies ran while one was open for 1% -> 0% of each run, Pallas kernels for 0% -> 0%
where the time goes in v2:
time: 43 us; the launch traced here: 42.5 us
  Pallas kernels  33.2 us (77%)
  local copies, waits for them, and re-layouts  8.05 us (19%)
  between operations  1.31 us (3%)
    pallas_call x1, Pallas kernels, kernel_shards(): pl.pallas_call(layer_kernel, out_shape=(jax.ShapeDtypeStruct(resid.shape,...  33.2 us
    unnamed x15, local copies, waits for them, and re-layouts  8.05 us

profile of v2, /device:TPU:0, one launch (start us, length us, event | category | flops | bytes accessed | tf_op | source)
XLA Modules:
  0.0 42.5 jit_solution(5058921383687501265)
XLA Ops:
  1.3 0.7 %copy.14.new_kv = bf16[2,1,1024]{2,1,0:T(2,128)(2,1)S(1)} copy(bf16[2,1,1024]{2,0,1:T(2,128)(2,1)} %param.14) | data formatting | bytes 8192 | tf_op args[3]
  2.0 0.8 %copy.13.choices = s32[16,2]{1,0:T(8,128)S(1)} copy(s32[16,2]{0,1:T(2,128)} %param.18) | data formatting | bytes 256 | tf_op args[7]
  2.7 1.6 %copy.15.router = bf16[6144,4]{1,0:T(8,128)(2,1)S(1)} copy(bf16[6144,4]{0,1:T(4,128)(2,1)} %param.17) | data formatting | bytes 98304 | tf_op args[6]
  4.3 0.0 copy-start
  4.3 0.9 %copy-done = bf16[2,1,64,1024]{3,2,1,0:T(8,128)(2,1)S(1)} copy-done((bf16[2,1,64,1024]{3,2,1,0:T(8,128)(2,1)S(1)}, bf16[2,1,64,1024]{3,2,1,0:T(8,128)(2,1)}, u32[]{:S(2)}) %copy-start) | copy-done | bytes 262168
  5.3 0.0 copy-start.1
  5.3 0.7 %copy-done.1 = bf16[1,6144]{1,0:T(2,128)(2,1)S(1)} copy-done((bf16[1,6144]{1,0:T(2,128)(2,1)S(1)}, bf16[1,6144]{1,0:T(2,128)(2,1)}, u32[]{:S(2)}) %copy-start.1) | copy-done | bytes 12312
  6.0 0.0 copy-start.2
  6.0 0.7 %copy-done.2 = bf16[1,6144]{1,0:T(2,128)(2,1)S(1)} copy-done((bf16[1,6144]{1,0:T(2,128)(2,1)S(1)}, bf16[1,6144]{1,0:T(2,128)(2,1)}, u32[]{:S(2)}) %copy-start.2) | copy-done | bytes 12312
  6.7 0.0 copy-start.3
  6.8 0.7 %copy-done.3 = f32[6144]{0:T(1024)S(1)} copy-done((f32[6144]{0:T(1024)S(1)}, f32[6144]{0:T(1024)}, u32[]{:S(2)}) %copy-start.3) | copy-done | bytes 24600
  7.5 0.0 copy-start.4
  7.5 0.7 %copy-done.4 = s32[16]{0:T(128)S(1)} copy-done((s32[16]{0:T(128)S(1)}, s32[16]{0:T(128)}, u32[]{:S(2)}) %copy-start.4) | copy-done | bytes 88
  8.1 33.2 %layer.1 = (bf16[1,6144]{1,0:T(2,128)(2,1)S(1)}, bf16[2,3072]{1,0:T(2,128)(2,1)S(1)}) custom-call(s32[1]{0:T(128)S(6)} %copy.18.lengths, s32[16,2]{1,0:T(8,128)S(1)} %copy.13.choices, s32[16]{0:T(128)S(1)} %copy-done.4, bf16[1,6144]{1,0:T(2,128)(2,1)S(1)} %copy-done.1, bf16[1,6144]{1,0:T(2,128)(2,1)S(1)} %copy-done.2, bf16[2,1,1024]{2,1,0:T(2,128)(2,1)S(1)} %copy.14.new_kv, ...), custom_call_target="tpu_custom_call" | custom-call | flops 805306368 | bytes 25165824 | tf_op jit(solution)/shard_map/layer/pallas_call | solution.py:514
  41.3 0.6 %copy.19 = bf16[1,6144]{1,0:T(2,128)(2,1)} copy(bf16[1,6144]{1,0:T(2,128)(2,1)S(1)} %get-tuple-element.4) | data formatting | bytes 24576
  41.9 0.6 %copy.20 = bf16[2,3072]{1,0:T(2,128)(2,1)} copy(bf16[2,3072]{1,0:T(2,128)(2,1)S(1)} %get-tuple-element.5) | data formatting | bytes 24576
Async XLA Ops:
  4.3 1.0 %copy-start = (bf16[2,1,64,1024]{3,2,1,0:T(8,128)(2,1)S(1)}, bf16[2,1,64,1024]{3,2,1,0:T(8,128)(2,1)}, u32[]{:S(2)}) copy-start(bf16[2,1,64,1024]{3,2,1,0:T(8,128)(2,1)} %cache.1) | copy-start | bytes 786436
  5.3 0.7 %copy-start.1 = (bf16[1,6144]{1,0:T(2,128)(2,1)S(1)}, bf16[1,6144]{1,0:T(2,128)(2,1)}, u32[]{:S(2)}) copy-start(bf16[1,6144]{1,0:T(2,128)(2,1)} %resid.1) | copy-start | bytes 36868
  6.0 0.7 %copy-start.2 = (bf16[1,6144]{1,0:T(2,128)(2,1)S(1)}, bf16[1,6144]{1,0:T(2,128)(2,1)}, u32[]{:S(2)}) copy-start(bf16[1,6144]{1,0:T(2,128)(2,1)} %query.1) | copy-start | bytes 36868
  6.7 0.7 %copy-start.3 = (f32[6144]{0:T(1024)S(1)}, f32[6144]{0:T(1024)}, u32[]{:S(2)}) copy-start(f32[6144]{0:T(1024)} %param.16) | copy-start | bytes 73732
  7.5 0.7 %copy-start.4 = (s32[16]{0:T(128)S(1)}, s32[16]{0:T(128)}, u32[]{:S(2)}) copy-start(s32[16]{0:T(128)} %overflow.1) | copy-start | bytes 196

commit v3 on v2

--- a/solution.py
+++ b/solution.py
@@ -124,6 +124,19 @@
 
 
 def layer_kernel(
+    lengths_at,
+    choices_at,
+    overflow_at,
+    resid_at,
+    query_at,
+    new_kv_at,
+    gain_at,
+    cache,
+    router,
+    up,
+    down,
+    stream_out,
+    moe_out,
     lengths,
     choices,
     overflow,
@@ -131,12 +144,6 @@
     query,
     new_kv,
     gain,
-    cache,
-    router,
-    up,
-    down,
-    stream_out,
-    moe_out,
     kv,
     rt,
     upw,
@@ -209,10 +216,35 @@
         other = lax.rem(block + k, BLOCKS)
         return other, other // CORES, lax.rem(other, CORES)
 
-    key_copy = pltpu.make_async_copy(cache.at[0, 0], kv.at[0], local_sem.at[0])
-    value_copy = pltpu.make_async_copy(cache.at[1, 0], kv.at[1], local_sem.at[1])
-    key_copy.start()
-    value_copy.start()
+    wanted = (
+        (query_at, query),
+        (cache.at[0, 0], kv.at[0]),
+        (lengths_at, lengths),
+        (new_kv_at, new_kv),
+        (cache.at[1, 0], kv.at[1]),
+        (resid_at, resid),
+        (gain_at, gain),
+        (choices_at, choices),
+        (overflow_at, overflow),
+        (router.at[:, pl.ds(pl.multiple_of(f * features, features), features)], rt),
+    )
+    small_copies = [
+        pltpu.make_async_copy(src, dst, local_sem.at[i]) for i, (src, dst) in enumerate(wanted)
+    ]
+    for copy in small_copies:
+        copy.start()
+    (
+        query_copy,
+        key_copy,
+        lengths_copy,
+        new_copy,
+        value_copy,
+        resid_copy,
+        gain_copy,
+        choices_copy,
+        overflow_copy,
+        router_copy,
+    ) = small_copies
 
     barrier = pltpu.get_barrier_semaphore()
     for k in range(1, PLANE):
@@ -222,10 +254,6 @@
         _, g2, t2 = block_peer(k)
         pl.semaphore_signal(barrier, inc=1, device_id=(g2, f, e, t2), device_id_type=MESH)
 
-    router_copy = pltpu.make_async_copy(
-        router.at[pl.ds(pl.multiple_of(f * features, features), features), :], rt, local_sem.at[2]
-    )
-
     def up_copy(c):
         start = pl.multiple_of(g * (UP_CHUNKS * hidden) + c * hidden, hidden)
         return pltpu.make_async_copy(up.at[0, pl.ds(start, hidden), :], upw.at[c], up_sem.at[c])
@@ -238,13 +266,14 @@
             down_sem.at[c],
         )
 
-    router_copy.start()
     for c in range(UP_CHUNKS):
         up_copy(c).start()
     for c in range(UP_CHUNKS):
         down_copy(c).start()
 
     qbd[...] = jnp.zeros_like(qbd)
+    query_copy.wait()
+    resid_copy.wait()
     query_row = query[...].astype(jnp.float32)
     resid_row = resid[...].astype(jnp.float32)
     for h in range(heads):
@@ -252,12 +281,14 @@
         qbd[h : h + 1, kv_at : kv_at + HEAD_SIZE] = query_row[:, h * HEAD_SIZE : (h + 1) * HEAD_SIZE]
         r48[h : h + 1, :] = resid_row[:, h * HEAD_SIZE : (h + 1) * HEAD_SIZE]
     inv_root = 1.0 / math.sqrt(HEAD_SIZE)
-    new_key = new_kv[0].astype(jnp.float32)
-    new_value = new_kv[1].astype(jnp.float32)
+    new_copy.wait()
+    new_rows = new_kv[...].astype(jnp.float32)
+    new_key, new_value = new_rows[0:1], new_rows[1:2]
     spread = qbd[...]
     own_score = jnp.sum(spread * new_key, axis=-1, keepdims=True) * inv_root
     spread = spread.astype(jnp.bfloat16)
     key_copy.wait()
+    lengths_copy.wait()
     scores = (
         lax.dot_general(
             spread, kv[0], (((1,), (1,)), ((), ())), preferred_element_type=jnp.float32
@@ -283,6 +314,7 @@
             attended,
         )
     levels = (r48[...] + attended).astype(jnp.bfloat16).astype(jnp.float32)
+    gain_copy.wait()
     total = jnp.sum(jnp.sum(levels * levels, axis=1, keepdims=True), axis=0, keepdims=True)
     normed = levels * lax.rsqrt(total / (heads * HEAD_SIZE) + 1e-05) * gain[...]
     filler = jnp.zeros((payload.shape[1] - pieces, HEAD_SIZE), jnp.float32)
@@ -311,12 +343,14 @@
     for h in range(heads):
         stream_out[:, h * HEAD_SIZE : (h + 1) * HEAD_SIZE] = levels[h : h + 1].astype(jnp.bfloat16)
 
+    choices_copy.wait()
+    overflow_copy.wait()
     at = lax.broadcasted_iota(jnp.int32, (16, HEAD_SIZE), 0)
     lane = lax.broadcasted_iota(jnp.int32, (16, HEAD_SIZE), 1)
     facts = jnp.zeros((16, HEAD_SIZE), jnp.float32)
     for row in range(16):
         place = row % 4 // 2 * 8 + row // 4 * 2 + row % 2
-        for col, value in enumerate((choices[row, 0], choices[row, 1], overflow[row])):
+        for col, value in enumerate((choices[0, row], choices[1, row], overflow[row])):
             facts = jnp.where((at == place) & (lane == col), value.astype(jnp.float32), facts)
     meta[g] = facts
     meta_copy = remote(
@@ -356,9 +390,11 @@
 
     across = (g, 1 - f, e, t)
     router_copy.wait()
-    labels = rt.shape[1]
+    labels = rt.shape[0]
     logit_mine[...] = jnp.zeros_like(logit_mine)
-    logit_mine[:, :labels] = jnp.dot(x[...], rt[...], preferred_element_type=jnp.float32)
+    logit_mine[:, :labels] = lax.dot_general(
+        x[...], rt[...], (((1,), (1,)), ((), ())), preferred_element_type=jnp.float32
+    )
     logit_copy = remote(logit_mine, logit_in, pair_send_sem.at[1], pair_recv_sem.at[1], across)
     logit_copy.start()
 
@@ -508,8 +544,7 @@
     kv_features = cache.shape[3]
     f32, bf16 = jnp.float32, jnp.bfloat16
     vmem = pl.BlockSpec(memory_space=pltpu.VMEM)
-    smem = pl.BlockSpec(memory_space=pltpu.SMEM)
-    anywhere = pl.BlockSpec(memory_space=pl.ANY)
+    hbm = pl.BlockSpec(memory_space=pltpu.HBM)
     dma = pltpu.SemaphoreType.DMA
     return pl.pallas_call(
         layer_kernel,
@@ -517,11 +552,18 @@
             jax.ShapeDtypeStruct(resid.shape, bf16),
             jax.ShapeDtypeStruct((ROWS // (BLOCKS * EXPERTS), features), bf16),
         ),
-        in_specs=[smem] * 3 + [vmem] * 4 + [anywhere] * 4,
+        in_specs=[hbm] * 11,
         out_specs=(vmem, vmem),
         scratch_shapes=[
+            pltpu.SMEM(lengths.shape, jnp.int32),
+            pltpu.SMEM(choices.shape[::-1], jnp.int32),
+            pltpu.SMEM(overflow.shape, jnp.int32),
+            pltpu.VMEM(resid.shape, bf16),
+            pltpu.VMEM(query.shape, bf16),
+            pltpu.VMEM((2, kv_features), bf16),
+            pltpu.VMEM((heads, HEAD_SIZE), f32),
             pltpu.VMEM((2, CACHE_POSITIONS, kv_features), bf16),
-            pltpu.VMEM((features, router_weight.shape[1]), bf16),
+            pltpu.VMEM((router_weight.shape[1], features), bf16),
             pltpu.VMEM((UP_CHUNKS, chunk, features), bf16),
             pltpu.VMEM((hidden, features), bf16),
             pltpu.VMEM((heads, kv_features), f32),
@@ -544,7 +586,7 @@
             pltpu.VMEM((OUT_CHUNKS, BLOCKS - 1, 16, width // 2), bf16),
             pltpu.VMEM((OUT_CHUNKS, EXPERTS, 2, width), f32),
             pltpu.VMEM((OUT_CHUNKS, EXPERTS - 1, 2, width), f32),
-            dma((3,)),
+            dma((10,)),
             dma((UP_CHUNKS,)),
             dma((UP_CHUNKS,)),
             dma((PLANE - 1,)),
@@ -561,7 +603,7 @@
             dma((OUT_CHUNKS * (EXPERTS - 1),)),
         ],
         compiler_params=pltpu.CompilerParams(
-            collective_id=0, has_side_effects=True, vmem_limit_bytes=48 * 1024 * 1024
+            collective_id=0, has_side_effects=True, vmem_limit_bytes=62 * 1024 * 1024
         ),
         cost_estimate=pl.CostEstimate(
             flops=4 * ROWS * hidden * features,
@@ -571,14 +613,14 @@
         name="layer",
     )(
         lengths,
-        choices,
+        choices.T,
         overflow,
         resid,
         query,
-        new_key_value,
+        new_key_value.reshape(2, kv_features),
         norm_gain.reshape(heads, HEAD_SIZE),
         cache,
-        router_weight,
+        router_weight.T,
         up_weight,
         down_weight,
     )

time: 43 us -> 37.1 us (0.86)
  local copies, waits for them, and re-layouts: 8.05 us -> 2.69 us
    unnamed x15 -> x2, local copies, waits for them, and re-layouts: 8.05 us -> 2.69 us
where the time goes in v3:
time: 37.1 us; the launch traced here: 36.8 us
  Pallas kernels  32.9 us (89%)
  local copies, waits for them, and re-layouts  2.69 us (7%)
  between operations  1.29 us (3%)
    pallas_call x1, Pallas kernels, kernel_shards(): pl.pallas_call(layer_kernel, out_shape=(jax.ShapeDtypeStruct(resid.shape,...  32.9 us
    unnamed x2, local copies, waits for them, and re-layouts  2.69 us

profile of v3, /device:TPU:0, one launch (start us, length us, event | category | flops | bytes accessed | tf_op | source)
XLA Modules:
  0.0 36.8 jit_solution(25072807681804727)
XLA Ops:
  1.3 32.9 %layer.1 = (bf16[1,6144]{1,0:T(2,128)(2,1)}, bf16[2,3072]{1,0:T(2,128)(2,1)}) custom-call(s32[1]{0:T(128)S(6)} %copy.15.lengths_at, s32[2,16]{1,0:T(2,128)} %bitcast.7, s32[16]{0:T(128)} %overflow_at.1, bf16[1,6144]{1,0:T(2,128)(2,1)} %resid_at.1, bf16[1,6144]{1,0:T(2,128)(2,1)} %query_at.1, bf16[2,1024]{1,0:T(2,128)(2,1)} %bitcast.6, f32[48,128]{1,0:T(8,128)} %bitcast.5, ...), custom_call_target="tpu_custom_call" | custom-call | flops 805306368 | bytes 25165824 | tf_op jit(solution)/shard_map/layer/pallas_call | solution.py:549
  34.2 1.4 %copy.16 = bf16[1,6144]{1,0:T(2,128)(2,1)} copy(bf16[1,6144]{1,0:T(2,128)(2,1)} %get-tuple-element.4) | data formatting | bytes 24576
  35.5 1.3 %copy.17 = bf16[2,3072]{1,0:T(2,128)(2,1)} copy(bf16[2,3072]{1,0:T(2,128)(2,1)} %get-tuple-element.5) | data formatting | bytes 24576

commit v4 on v3

--- a/solution.py
+++ b/solution.py
@@ -166,6 +166,7 @@
     own_out,
     a_send,
     a_in,
+    z_mine,
     z_send,
     z_in,
     local_sem,
@@ -389,6 +390,22 @@
         )
 
     across = (g, 1 - f, e, t)
+    def pre_copy(c):
+        return remote(
+            pre_send.at[c], pre_in.at[c], pre_send_sem.at[c], pre_recv_sem.at[c], across
+        )
+
+    def up_step(c, carry):
+        up_copy(c).wait()
+        partial = lax.dot_general(
+            x[...], upw[c], (((1,), (1,)), ((), ())), preferred_element_type=jnp.float32
+        )
+        pre_mine[c] = partial
+        pre_send[c] = partial.astype(jnp.bfloat16)
+        pre_copy(c).start()
+        return carry
+
+    up_step(0, 0)
     router_copy.wait()
     labels = rt.shape[0]
     logit_mine[...] = jnp.zeros_like(logit_mine)
@@ -397,23 +414,7 @@
     )
     logit_copy = remote(logit_mine, logit_in, pair_send_sem.at[1], pair_recv_sem.at[1], across)
     logit_copy.start()
-
-    def pre_copy(c):
-        return remote(
-            pre_send.at[c], pre_in.at[c], pre_send_sem.at[c], pre_recv_sem.at[c], across
-        )
-
-    def up_step(c, carry):
-        up_copy(c).wait()
-        partial = lax.dot_general(
-            x[...], upw[c], (((1,), (1,)), ((), ())), preferred_element_type=jnp.float32
-        )
-        pre_mine[c] = partial
-        pre_send[c] = partial.astype(jnp.bfloat16)
-        pre_copy(c).start()
-        return carry
-
-    lax.fori_loop(0, UP_CHUNKS, up_step, 0)
+    lax.fori_loop(1, UP_CHUNKS, up_step, 0)
 
     meta_copy.wait_recv()
     logit_copy.wait_recv()
@@ -438,16 +439,13 @@
             jnp.bfloat16
         )
 
-    split = UP_CHUNKS // 2 * hidden
-    for c in range(UP_CHUNKS // 2):
+    split = (UP_CHUNKS - 1) * hidden
+    for c in range(UP_CHUNKS - 1):
         activate(c)
-    for n in range(OUT_CHUNKS):
-        cols = slice(n * width, (n + 1) * width)
-        acc[:, cols] = jnp.dot(
-            act[:, :split], downw[:split, cols], preferred_element_type=jnp.float32
-        )
-    for c in range(UP_CHUNKS // 2, UP_CHUNKS):
-        activate(c)
+        rows = slice(c * hidden, (c + 1) * hidden)
+        product = jnp.dot(act[:, rows], downw[rows, :], preferred_element_type=jnp.float32)
+        acc[...] = product if c == 0 else acc[...] + product
+    activate(UP_CHUNKS - 1)
 
     a_copies = [[] for _ in range(OUT_CHUNKS)]
     z_copies = [[] for _ in range(OUT_CHUNKS)]
@@ -484,8 +482,11 @@
             a_copies[n][k - 1].wait_recv()
             value = value + a_in[n, k - 1].astype(jnp.float32)
         for to in range(EXPERTS):
-            z_send[n, to, :, :half] = value[2 * to : 2 * to + 2]
-            z_send[n, to, :, half:] = value[PLANE + 2 * to : PLANE + 2 * to + 2]
+            for j in range(width // HEAD_SIZE):
+                side, col = divmod(j * HEAD_SIZE, half)
+                row = side * PLANE + 2 * to
+                z_mine[n, to, 2 * j : 2 * j + 2, :] = value[row : row + 2, col : col + HEAD_SIZE]
+            z_send[n, to] = z_mine[n, to].astype(jnp.bfloat16)
         for k in range(1, EXPERTS):
             e2 = lax.rem(e + k, EXPERTS)
             at_sem = n * (EXPERTS - 1) + k - 1
@@ -502,15 +503,16 @@
 
     for n in range(OUT_CHUNKS):
         multiply(n)
-        if n > 0:
-            add_blocks(n - 1)
-    add_blocks(OUT_CHUNKS - 1)
     for n in range(OUT_CHUNKS):
-        value = z_send[n, e]
+        add_blocks(n)
+    for n in range(OUT_CHUNKS):
+        value = z_mine[n, e]
         for k in range(1, EXPERTS):
             z_copies[n][k - 1].wait_recv()
-            value = value + z_in[n, k - 1]
-        moe_out[:, n * width : (n + 1) * width] = value.astype(jnp.bfloat16)
+            value = value + z_in[n, k - 1].astype(jnp.float32)
+        for j in range(width // HEAD_SIZE):
+            at_col = n * width + j * HEAD_SIZE
+            moe_out[:, at_col : at_col + HEAD_SIZE] = value[2 * j : 2 * j + 2].astype(jnp.bfloat16)
 
     for copy in row_copies + block_copies + [meta_copy, logit_copy]:
         copy.wait_send()
@@ -538,6 +540,7 @@
     hidden = hidden_all // GROUPS
     chunk = hidden // UP_CHUNKS
     width = features // OUT_CHUNKS
+    fold = 2 * width // HEAD_SIZE
     pieces = features // HEAD_SIZE
     padded = -(-pieces // 16) * 16
     heads = FSDP * pieces
@@ -584,8 +587,9 @@
             pltpu.VMEM((BLOCKS, 16, width // 2), f32),
             pltpu.VMEM((OUT_CHUNKS, BLOCKS, 16, width // 2), bf16),
             pltpu.VMEM((OUT_CHUNKS, BLOCKS - 1, 16, width // 2), bf16),
-            pltpu.VMEM((OUT_CHUNKS, EXPERTS, 2, width), f32),
-            pltpu.VMEM((OUT_CHUNKS, EXPERTS - 1, 2, width), f32),
+            pltpu.VMEM((OUT_CHUNKS, EXPERTS, fold, HEAD_SIZE), f32),
+            pltpu.VMEM((OUT_CHUNKS, EXPERTS, fold, HEAD_SIZE), bf16),
+            pltpu.VMEM((OUT_CHUNKS, EXPERTS - 1, fold, HEAD_SIZE), bf16),
             dma((10,)),
             dma((UP_CHUNKS,)),
             dma((UP_CHUNKS,)),

time: 37.1 us -> 34 us (0.916)
  Pallas kernels: 32.9 us -> 29.8 us
    pallas_call x1, Pallas kernels: 32.9 us -> 29.8 us  [kernel_shards(): pl.pallas_call(layer_kernel, out_shape=(jax.ShapeDtypeStruct(resid.shape,...]
where the time goes in v4:
time: 34 us; the launch traced here: 33.7 us
  Pallas kernels  29.8 us (88%)
  local copies, waits for them, and re-layouts  2.69 us (8%)
  between operations  1.29 us (4%)
    pallas_call x1, Pallas kernels, kernel_shards(): pl.pallas_call(layer_kernel, out_shape=(jax.ShapeDtypeStruct(resid.shape,...  29.8 us
    unnamed x2, local copies, waits for them, and re-layouts  2.69 us

profile of v4, /device:TPU:0, one launch (start us, length us, event | category | flops | bytes accessed | tf_op | source)
XLA Modules:
  0.0 33.7 jit_solution(11115524533239801744)
XLA Ops:
  1.3 29.8 %layer.1 = (bf16[1,6144]{1,0:T(2,128)(2,1)}, bf16[2,3072]{1,0:T(2,128)(2,1)}) custom-call(s32[1]{0:T(128)S(6)} %copy.15.lengths_at, s32[2,16]{1,0:T(2,128)} %bitcast.7, s32[16]{0:T(128)} %overflow_at.1, bf16[1,6144]{1,0:T(2,128)(2,1)} %resid_at.1, bf16[1,6144]{1,0:T(2,128)(2,1)} %query_at.1, bf16[2,1024]{1,0:T(2,128)(2,1)} %bitcast.6, f32[48,128]{1,0:T(8,128)} %bitcast.5, ...), custom_call_target="tpu_custom_call" | custom-call | flops 805306368 | bytes 25165824 | tf_op jit(solution)/shard_map/layer/pallas_call | solution.py:552
  31.1 1.4 %copy.16 = bf16[1,6144]{1,0:T(2,128)(2,1)} copy(bf16[1,6144]{1,0:T(2,128)(2,1)} %get-tuple-element.4) | data formatting | bytes 24576
  32.4 1.3 %copy.17 = bf16[2,3072]{1,0:T(2,128)(2,1)} copy(bf16[2,3072]{1,0:T(2,128)(2,1)} %get-tuple-element.5) | data formatting | bytes 24576

commit v5 on v4

--- a/solution.py
+++ b/solution.py
@@ -135,8 +135,7 @@
     router,
     up,
     down,
-    stream_out,
-    moe_out,
+    both_out,
     lengths,
     choices,
     overflow,
@@ -196,7 +195,7 @@
     heads = 2 * pieces
     group_heads = heads // KEY_VALUE_HEADS
     hidden = upw.shape[1]
-    width = moe_out.shape[1] // OUT_CHUNKS
+    width = features // OUT_CHUNKS
     half = width // 2
 
     def remote(src, dst, send, recv, device):
@@ -342,7 +341,7 @@
     rows_in[here] = payload[f]
 
     for h in range(heads):
-        stream_out[:, h * HEAD_SIZE : (h + 1) * HEAD_SIZE] = levels[h : h + 1].astype(jnp.bfloat16)
+        both_out[0:1, h * HEAD_SIZE : (h + 1) * HEAD_SIZE] = levels[h : h + 1].astype(jnp.bfloat16)
 
     choices_copy.wait()
     overflow_copy.wait()
@@ -512,7 +511,11 @@
             value = value + z_in[n, k - 1].astype(jnp.float32)
         for j in range(width // HEAD_SIZE):
             at_col = n * width + j * HEAD_SIZE
-            moe_out[:, at_col : at_col + HEAD_SIZE] = value[2 * j : 2 * j + 2].astype(jnp.bfloat16)
+            for row in range(2):
+                to = row * features + at_col
+                both_out[1:2, to : to + HEAD_SIZE] = value[2 * j + row : 2 * j + row + 1].astype(
+                    jnp.bfloat16
+                )
 
     for copy in row_copies + block_copies + [meta_copy, logit_copy]:
         copy.wait_send()
@@ -549,14 +552,11 @@
     vmem = pl.BlockSpec(memory_space=pltpu.VMEM)
     hbm = pl.BlockSpec(memory_space=pltpu.HBM)
     dma = pltpu.SemaphoreType.DMA
-    return pl.pallas_call(
+    both = pl.pallas_call(
         layer_kernel,
-        out_shape=(
-            jax.ShapeDtypeStruct(resid.shape, bf16),
-            jax.ShapeDtypeStruct((ROWS // (BLOCKS * EXPERTS), features), bf16),
-        ),
+        out_shape=jax.ShapeDtypeStruct((2, FSDP * features), bf16),
         in_specs=[hbm] * 11,
-        out_specs=(vmem, vmem),
+        out_specs=vmem,
         scratch_shapes=[
             pltpu.SMEM(lengths.shape, jnp.int32),
             pltpu.SMEM(choices.shape[::-1], jnp.int32),
@@ -628,6 +628,7 @@
         up_weight,
         down_weight,
     )
+    return both[0:1], both[1:2].reshape(2, features)
 
 
 def solution(mesh):

time: 34 us -> 33.2 us (0.976)
  local copies, waits for them, and re-layouts: 2.69 us -> 2.08 us
    unnamed x2 -> x0, local copies, waits for them, and re-layouts: 2.69 us -> none
    slice x0 -> x1, local copies, waits for them, and re-layouts: none -> 1.47 us  [kernel_shards(): return (both[0:1], both[1:2].reshape(2, features))]
    reshape x0 -> x1, local copies, waits for them, and re-layouts: none -> 0.61 us  [kernel_shards(): return (both[0:1], both[1:2].reshape(2, features))]
where the time goes in v5:
time: 33.2 us; the launch traced here: 33 us
  Pallas kernels  29.6 us (89%)
  local copies, waits for them, and re-layouts  2.08 us (6%)
  between operations  1.29 us (4%)
    pallas_call x1, Pallas kernels, kernel_shards(): pl.pallas_call(layer_kernel, out_shape=jax.ShapeDtypeStruct((2, FSDP * fe...  29.6 us
    slice x1, local copies, waits for them, and re-layouts, kernel_shards(): return (both[0:1], both[1:2].reshape(2, features))  1.47 us

profile of v5, /device:TPU:0, one launch (start us, length us, event | category | flops | bytes accessed | tf_op | source)
XLA Modules:
  0.0 33.0 jit_solution(11645174023557738047)
XLA Ops:
  1.3 29.6 %layer.1 = bf16[2,6144]{1,0:T(2,128)(2,1)} custom-call(s32[1]{0:T(128)S(6)} %copy.13.lengths_at, s32[2,16]{1,0:T(2,128)} %bitcast.7, s32[16]{0:T(128)} %overflow_at.1, bf16[1,6144]{1,0:T(2,128)(2,1)} %resid_at.1, bf16[1,6144]{1,0:T(2,128)(2,1)} %query_at.1, bf16[2,1024]{1,0:T(2,128)(2,1)} %bitcast.6, f32[48,128]{1,0:T(8,128)} %bitcast.5, ...), custom_call_target="tpu_custom_call" | custom-call | flops 805306368 | bytes 25165824 | tf_op jit(solution)/shard_map/layer/pallas_call | solution.py:555
  30.9 1.5 %slice_reduce_fusion = (bf16[6144]{0:T(1024)(128)(2,1)S(1)}, bf16[1,6144]{1,0:T(2,128)(2,1)}) fusion(bf16[2,6144]{1,0:T(2,128)(2,1)} %layer.1), kind=kLoop, calls=%fused_computation | loop fusion | bytes 49152 | tf_op jit(solution)/shard_map/slice | solution.py:631
  32.4 0.6 %reshape.15 = bf16[2,3072]{1,0:T(2,128)(2,1)} reshape(bf16[6144]{0:T(1024)(128)(2,1)S(1)} %get-tuple-element.2) | data formatting | bytes 24576 | tf_op jit(solution)/shard_map/reshape | solution.py:631
